TPU v7x, 32 devices: a whole 2x2x4 slice. The times are simulated.
32 devices in a mesh: clu: 8 (over z, x), grp: 4 (over y, core).
Axes of the slice: x: 2, y: 2, z: 4, core: 2. Of those that a mesh axis runs over, the one named last changes fastest.
Arguments:
- tokens: bfloat16 [32768, 1024], P(('clu', 'grp')), may hold values from -6 to 6
- segment_ids: int32 [32, 1024], P(('clu', 'grp')), may hold values from 0 to 127, never falling along the last dimension, each value on 1 to 32 neighbouring positions
- w_in: bfloat16 [1024, 2048], replicated, may hold values from -0.1875 to 0.1875
- b_in: float32 [2048], replicated, may hold values from -4 to 4
- w_out: bfloat16 [2048, 1024], replicated, may hold values from -0.125 to 0.125
- b_out: float32 [1024], replicated, may hold values from -1.5 to 1.5
- owner_ids: int32 [4096, 1], P(('clu', 'grp')), may hold values from 0 to 7; in each aligned block of 128 rows (0 to 127, 128 to 255, ...) at most 32 rows name the same one
- sub_ids: int32 [4096], P(('clu', 'grp')), may hold values from 0 to 255
Outputs:
- pooled: bfloat16 [4096, 1024], P(('clu', 'grp'))
- nearest: float32 [4096], P(('clu', 'grp'))
Inputs may be any that keep to these rules, and one draw needn't show every extreme that they name: `owner_ids`: no device holds more than 32 documents of one owner; some device holds exactly 32. `segment_ids`: each row lists documents 0 to 127 in order, each on 1 to 32 consecutive positions, one on exactly 32.
All inputs are finite; a program needn't handle non-finite values.
Results may differ from a plain program's by a relative error of at most 0.0043.
Values may be sent and summed in bfloat16 or wider, within the bound.
A program may use at most 64 MiB of HBM per device.

v0:
```python
import jax
import jax.numpy as jnp
from jax import lax
from jax.sharding import PartitionSpec as P


def encode(token_block, segments, w_in, b_in, w_out, b_out, doc_count):
    pre_act = jnp.dot(token_block, w_in, preferred_element_type=jnp.float32) + b_in
    activated = jax.nn.gelu(pre_act, approximate=False).astype(jnp.bfloat16)
    layer_out = (
        token_block.astype(jnp.float32)
        + jnp.dot(activated, w_out, preferred_element_type=jnp.float32)
        + b_out
    ).astype(jnp.bfloat16)
    member = segments[None, :] == jnp.arange(doc_count, dtype=jnp.int32)[:, None]
    totals = jnp.dot(member.astype(jnp.bfloat16), layer_out, preferred_element_type=jnp.float32)
    counts = jnp.sum(member.astype(jnp.float32), axis=1, keepdims=True)
    mean_rows = totals / counts
    scale_inv = lax.rsqrt(jnp.sum(mean_rows * mean_rows, axis=1, keepdims=True) + 1e-06)
    return (mean_rows.astype(jnp.bfloat16), (mean_rows * scale_inv).astype(jnp.bfloat16))


def absorb(best_sim, own_units, own_meta, piece_units, piece_meta):
    similar = lax.dot_general(
        own_units, piece_units, (((1,), (1,)), ((), ())), preferred_element_type=jnp.float32
    )
    own_key = own_meta[:, 1][:, None]
    matched = (
        (own_key == piece_meta[:, 1][None, :])
        & (own_key >= 0)
        & (own_meta[:, 0][:, None] != piece_meta[:, 0][None, :])
    )
    return jnp.maximum(best_sim, jnp.max(jnp.where(matched, similar, -1.0), axis=1))


def per_device(tokens, segment_ids, w_in, b_in, w_out, b_out, owner_ids, sub_ids):
    n_clu = lax.axis_size("clu")
    n_grp = lax.axis_size("grp")
    doc_count = owner_ids.shape[0]
    model_width = tokens.shape[1]
    capacity = 2 * doc_count // n_clu
    own_count = n_clu * capacity
    pooled, unit_rows = encode(tokens, segment_ids[0], w_in, b_in, w_out, b_out, doc_count)
    owner_rank = owner_ids[:, 0]
    owner_hits = (owner_rank[:, None] == jnp.arange(n_clu, dtype=jnp.int32)[None, :]).astype(
        jnp.int32
    )
    before = jnp.cumsum(owner_hits, axis=0) - owner_hits
    slot_index = jnp.sum(before * owner_hits, axis=1)
    slot_place = owner_rank * capacity + slot_index
    grp_index = lax.axis_index("grp")
    device_rank = lax.axis_index("clu") * n_grp + grp_index
    doc_index = device_rank * doc_count + jnp.arange(doc_count, dtype=jnp.int32)
    start_best = jnp.full((own_count,), -1.0, jnp.float32)
    doc_info = jnp.stack([slot_place, doc_index, sub_ids], axis=1)
    every_unit, every_info = (
        lax.all_gather(unit_rows, "grp", axis=0, tiled=True),
        lax.all_gather(doc_info, "grp", axis=0, tiled=True),
    )
    source_grp = jnp.arange(n_grp * doc_count, dtype=jnp.int32) // doc_count
    wide_place = (
        every_info[:, 0] // capacity * (n_grp * capacity)
        + source_grp * capacity
        + every_info[:, 0] % capacity
    )
    send_units = (
        jnp.zeros((n_clu * n_grp * capacity, model_width), jnp.bfloat16)
        .at[wide_place]
        .set(every_unit)
    )
    send_meta = (
        jnp.full((n_clu * n_grp * capacity, 2), -1, jnp.int32).at[wide_place].set(every_info[:, 1:])
    )
    got_units, got_meta = (
        lax.all_to_all(
            send_units.reshape(n_clu, n_grp * capacity, model_width),
            "clu",
            split_axis=0,
            concat_axis=0,
            tiled=True,
        ),
        lax.all_to_all(
            send_meta.reshape(n_clu, n_grp * capacity, 2),
            "clu",
            split_axis=0,
            concat_axis=0,
            tiled=True,
        ),
    )
    own_units = lax.dynamic_slice_in_dim(
        got_units.reshape(n_clu, n_grp, capacity, model_width), grp_index, 1, 1
    ).reshape(own_count, model_width)
    own_meta = lax.dynamic_slice_in_dim(
        got_meta.reshape(n_clu, n_grp, capacity, 2), grp_index, 1, 1
    ).reshape(own_count, 2)
    best_sim = absorb(
        start_best,
        own_units,
        own_meta,
        got_units.reshape(n_clu * n_grp * capacity, model_width),
        got_meta.reshape(n_clu * n_grp * capacity, 2),
    )
    returned = lax.all_to_all(
        best_sim.reshape(n_clu, capacity), "clu", split_axis=0, concat_axis=0, tiled=True
    )
    nearest = jnp.take(returned.reshape(own_count), slot_place)
    return (pooled, nearest)


def solution(mesh):
    in_specs = (
        P(("clu", "grp"), None),
        P(("clu", "grp"), None),
        P(),
        P(),
        P(),
        P(),
        P(("clu", "grp"), None),
        P(("clu", "grp")),
    )
    out_specs = (P(("clu", "grp"), None), P(("clu", "grp")))
    return jax.shard_map(
        per_device, mesh=mesh, in_specs=in_specs, out_specs=out_specs, check_vma=False
    )
```

profile of v0, /device:TPU:0, one launch (start us, length us, event | category | flops | bytes accessed | tf_op | source)
XLA Modules:
  0.0 142.4 jit_solution(7249988245750855850)
XLA Ops:
  7.2 0.0 all-gather.2.cloned.1.call-start
  7.2 0.8 convert_reduce_fusion
  8.0 0.0 copy-start
  8.0 0.0 copy-start.1
  8.0 0.0 copy-start.3
  8.1 30.1 %fusion.10 = f32[1024,1024]{1,0:T(8,128)} fusion(bf16[2048,1024]{1,0:T(8,128)(2,1)} %param.12, f32[2048]{0:T(1024)} %param.11, bf16[1024,1024]{1,0:T(8,128)(2,1)} %param.8, bf16[1024,2048]{1,0:T(8,128)(2,1)} %param.10), kind=kOutput, calls=%fused_computation.23 | convolution fusion | flops 8728346624 | bytes 14688256 | tf_op jit(solution)/shard_map/dot_general | solution.py:12
  38.2 0.0 copy-done
  38.2 0.0 copy-done.1
  38.2 0.0 copy-done.3
  38.2 0.0 copy-start.2
  38.2 0.0 copy-start.4
  38.2 3.1 %multiply_reduce_fusion = (f32[128]{0:T(128)S(1)}, f32[128,1024]{1,0:T(8,128)S(1)}) fusion(f32[128]{0:T(128)S(1)} %convert_reduce_fusion, f32[1024,1024]{1,0:T(8,128)} %fusion.10, bf16[1024,1024]{1,0:T(8,128)(2,1)S(1)} %copy-done, f32[1024]{0:T(1024)S(1)} %copy-done.3, s32[1024]{0:T(1024)S(1)} %bitcast.38), kind=kOutput, calls=%fused_computation.33 | convolution fusion | flops 273153920 | bytes 6824960 | tf_op jit(solution)/shard_map/dot_general | solution.py:16
  41.3 0.8 multiply_convert_fusion
  42.1 0.0 all-gather.2.cloned.1.call-update
  42.2 0.0 copy-done.2
  42.2 0.1 fusion.23
  42.3 0.2 reduce_window_sum.11
  42.4 0.2 select_reduce_fusion
  42.6 0.0 copy-done.4
  42.7 6.4 %all_gather.6 = s32[512,3]{0,1:T(4,128)S(1)} all-gather(s32[128,3]{0,1:T(4,128)S(1)} %pad_add_fusion), channel_id=1, replica_groups=mesh['clu'=8,'grp'=4] {'grp'}, dimensions={0}, use_global_device_ids=true | all-gather | bytes 7680 | tf_op jit(solution)/shard_map/all_gather | solution.py:58
  49.0 0.2 copy.16
  49.2 1.8 %scatter_custom_fusion = s32[1024,2]{1,0:T(8,128)S(1)} fusion(s32[512]{0:T(512)S(1)} %bitcast.43, s32[512,2]{1,0:T(8,128)S(1)} %copy.16, s32[]{:T(128)} %constant.134.clone.1), kind=kCustom, calls=%fused_computation.36 | custom fusion | bytes 8196 | tf_op jit(solution)/shard_map/scatter | solution.py:72
  51.1 0.8 copy.17
  51.8 6.3 %all-to-all-start = ((s32[8,128,2]{1,2,0:T(2,128)}), s32[8,128,2]{1,2,0:T(2,128)S(1)}, u32[]{:S(2)}, u32[]{:S(2)}) async-start(s32[8,128,2]{1,2,0:T(2,128)} %copy.17), calls=%async_computation | async-start | bytes 16384 | tf_op jit(solution)/shard_map/all_to_all | solution.py:82
  58.1 3.6 %all-gather.2.cloned.1.call-done = bf16[512,1024]{1,0:T(8,128)(2,1)} async-done(((bf16[128,1024]{1,0:T(8,128)(2,1)}), bf16[512,1024]{1,0:T(8,128)(2,1)}) %all-gather.2.cloned.1.call-update) | async-done | bytes 1048592 | tf_op jit(solution)/shard_map/all_gather | solution.py:57
  61.7 4.8 %scatter_custom_fusion.1 = bf16[1024,1024]{1,0:T(8,128)(2,1)} fusion(s32[512]{0:T(512)S(1)} %bitcast.44, bf16[512,1024]{1,0:T(8,128)(2,1)} %all-gather.2.cloned.1.call-done, bf16[]{:T(256)} %constant.146.clone.1), kind=kCustom, calls=%fused_computation.30 | custom fusion | bytes 2097664 | tf_op jit(solution)/shard_map/scatter | solution.py:69
  66.5 0.0 all-to-all-done
  66.6 5.5 %all-to-all-start.1 = ((bf16[8,128,1024]{2,1,0:T(8,128)(2,1)}), bf16[8,128,1024]{2,1,0:T(8,128)(2,1)S(1)}, u32[]{:S(2)}, u32[]{:S(2)}) async-start(bf16[8,128,1024]{2,1,0:T(8,128)(2,1)} %bitcast.12), calls=%async_computation.1 | async-start | bytes 4194304 | tf_op jit(solution)/shard_map/all_to_all | solution.py:75
  72.1 0.1 reshape.111
  72.2 0.1 reshape.112
  72.3 48.4 %all-to-all-done.1 = bf16[8,128,1024]{2,1,0:T(8,128)(2,1)S(1)} async-done(((bf16[8,128,1024]{2,1,0:T(8,128)(2,1)}), bf16[8,128,1024]{2,1,0:T(8,128)(2,1)S(1)}, u32[]{:S(2)}, u32[]{:S(2)}) %all-to-all-start.1) | async-done | bytes 2097184 | tf_op jit(solution)/shard_map/all_to_all | solution.py:75
  120.8 0.9 fusion.16
  121.7 0.7 max_broadcast_in_dim.15
  122.4 3.6 %all-to-all-start.2 = ((f32[8,1,32]{2,1,0:T(1,128)}), f32[8,1,32]{2,1,0:T(1,128)S(1)}, u32[]{:S(2)}, u32[]{:S(2)}) async-start(f32[8,1,32]{2,1,0:T(1,128)} %max_broadcast_in_dim.15), calls=%async_computation.2 | async-start | bytes 8192 | tf_op jit(solution)/shard_map/all_to_all | solution.py:103
  126.0 6.5 %all-to-all-done.2 = f32[8,1,32]{2,1,0:T(1,128)S(1)} async-done(((f32[8,1,32]{2,1,0:T(1,128)}), f32[8,1,32]{2,1,0:T(1,128)S(1)}, u32[]{:S(2)}, u32[]{:S(2)}) %all-to-all-start.2) | async-done | bytes 1056 | tf_op jit(solution)/shard_map/all_to_all | solution.py:103
  132.5 0.5 broadcast.139
  133.0 0.7 reduce.5
  133.7 0.1 reshape.118
  133.8 1.3 gather_fusion
  135.0 0.5 bitcast_select_fusion
  (13 shorter events, 0.2 us)
Async XLA Ops:
  7.2 54.6 %all-gather.2.cloned.1.call-start = ((), (), s32[]{:S(2)}) async-start(), calls=%async_computation.3 | async-start | bytes 1310720 | tf_op jit(solution)/shard_map/all_gather | solution.py:57
  8.0 30.2 %copy-start = (bf16[1024,1024]{1,0:T(8,128)(2,1)S(1)}, bf16[1024,1024]{1,0:T(8,128)(2,1)}, u32[]{:S(2)}) copy-start(bf16[1024,1024]{1,0:T(8,128)(2,1)} %param.8) | copy-start | bytes 6291460
  8.0 30.2 %copy-start.1 = (s32[1,1024]{1,0:T(1,128)S(1)}, s32[1,1024]{1,0:T(1,128)}, u32[]{:S(2)}) copy-start(s32[1,1024]{1,0:T(1,128)} %param.9) | copy-start | bytes 12292
  8.0 30.2 %copy-start.3 = (f32[1024]{0:T(1024)S(1)}, f32[1024]{0:T(1024)}, u32[]{:S(2)}) copy-start(f32[1024]{0:T(1024)} %param.13) | copy-start | bytes 12292
  38.2 4.0 %copy-start.2 = (s32[128,1]{0,1:T(1,128)S(1)}, s32[128,1]{0,1:T(1,128)}, u32[]{:S(2)}) copy-start(s32[128,1]{0,1:T(1,128)} %param.14) | copy-start | bytes 1540
  38.2 4.4 %copy-start.4 = (s32[128]{0:T(128)S(1)}, s32[128]{0:T(128)}, u32[]{:S(2)}) copy-start(s32[128]{0:T(128)} %param.15) | copy-start | bytes 1540
  51.8 14.7 %all-to-all-start = ((s32[8,128,2]{1,2,0:T(2,128)}), s32[8,128,2]{1,2,0:T(2,128)S(1)}, u32[]{:S(2)}, u32[]{:S(2)}) async-start(s32[8,128,2]{1,2,0:T(2,128)} %copy.17), calls=%async_computation | async-start | bytes 16384 | tf_op jit(solution)/shard_map/all_to_all | solution.py:82
  66.6 54.2 %all-to-all-start.1 = ((bf16[8,128,1024]{2,1,0:T(8,128)(2,1)}), bf16[8,128,1024]{2,1,0:T(8,128)(2,1)S(1)}, u32[]{:S(2)}, u32[]{:S(2)}) async-start(bf16[8,128,1024]{2,1,0:T(8,128)(2,1)} %bitcast.12), calls=%async_computation.1 | async-start | bytes 4194304 | tf_op jit(solution)/shard_map/all_to_all | solution.py:75
  122.4 10.1 %all-to-all-start.2 = ((f32[8,1,32]{2,1,0:T(1,128)}), f32[8,1,32]{2,1,0:T(1,128)S(1)}, u32[]{:S(2)}, u32[]{:S(2)}) async-start(f32[8,1,32]{2,1,0:T(1,128)} %max_broadcast_in_dim.15), calls=%async_computation.2 | async-start | bytes 8192 | tf_op jit(solution)/shard_map/all_to_all | solution.py:103
Sparse Core Ops, SparseCore 0:
  42.3 19.3 all-gather.1
where the time goes:
time: 143 us; the launch traced here: 142 us
  waiting for transfers between devices  58.5 us (41%)
  matrix products  34.1 us (24%)
  starting transfers between devices  15.5 us (11%)
  between operations  14.2 us (10%)
  local copies, waits for them, and re-layouts  10.4 us (7%)
  blocking collectives  6.36 us (4%)
  other arithmetic  3.35 us (2%)
    all_to_all x1, waiting for transfers between devices, per_device(): lax.all_to_all(send_units.reshape(n_clu, n_grp * capacity, model_width),...  48.4 us
    dot_general x1, matrix products, encode(): jnp.dot(activated, w_out, preferred_element_type=jnp.float32)  30.1 us
    all_to_all x1, waiting for transfers between devices, per_device(): lax.all_to_all(best_sim.reshape(n_clu, capacity), 'clu', split_axis=0, co...  6.46 us
    all_gather x1, blocking collectives, per_device(): lax.all_gather(doc_info, 'grp', axis=0, tiled=True)  6.36 us
    all_to_all x1, starting transfers between devices, per_device(): lax.all_to_all(send_meta.reshape(n_clu, n_grp * capacity, 2), 'clu', spli...  6.26 us
    all_to_all x1, starting transfers between devices, per_device(): lax.all_to_all(send_units.reshape(n_clu, n_grp * capacity, model_width),...  5.53 us
    scatter x1, local copies, waits for them, and re-layouts, per_device(): send_units = jnp.zeros((n_clu * n_grp * capacity, model_width), jnp.bfloa...  4.82 us
    all_to_all x1, starting transfers between devices, per_device(): lax.all_to_all(best_sim.reshape(n_clu, capacity), 'clu', split_axis=0, co...  3.64 us
  transfers between devices with their start and end apart: 4, of which 3 were waited for; matrix products, arithmetic and copies ran while one was open for 6% of the time, Pallas kernels for 0%

commit v1 on v0

v1 whole, which is shorter than its diff:
```python
import functools
import jax
import jax.numpy as jnp
from jax import lax
from jax.experimental import pallas as pl
from jax.experimental.pallas import tpu as pltpu
from jax.sharding import PartitionSpec as P

MESH = pl.DeviceIdType.MESH
F32 = jnp.float32
BF16 = jnp.bfloat16
META = 128
HI = 32
LO = 16


def gelu(x):
    return 0.5 * x * (1.0 + lax.erf(x * 0.7071067811865476))


def dot_nt(a, b):
    return lax.dot_general(a, b, (((1,), (1,)), ((), ())), preferred_element_type=F32)


def kernel(
    n_clu, n_grp, cap, parts,
    tok_hbm, seg_ref, w_in_hbm, b_in_ref, w_out_hbm, b_out_ref, owner_ref, sub_ref,
    pooled_ref, near_ref,
    tok, w_in, w_out, act, member, place, send, send_meta, gath, gath_meta, ret_out, ret_in,
    tok_sem, win_sem, wout_sem, a_send, a_recv, f_send, f_recv, r_send, r_recv,
):
    rows_n, width = tok.shape
    ff = w_in.shape[1]
    docs = pooled_ref.shape[0]
    slots = n_clu * cap
    col = width // parts
    n_y = n_grp // 2
    clu = lax.axis_index("clu")
    grp = lax.axis_index("grp")
    y_at, core = grp // 2, lax.rem(grp, 2)
    sib = y_at * 2 + 1 - core

    def peer(k):
        return lax.rem(clu + k, n_clu)

    def y_peer(t):
        return lax.rem(y_at + t, n_y) * 2 + core

    def y_source(t):
        return lax.rem(y_at + n_y - t, n_y) * 2 + core

    def y_source_sib(t):
        return lax.rem(y_at + n_y - t, n_y) * 2 + 1 - core

    f_parts = win_sem.shape[0]
    f_col = ff // f_parts

    def w_in_copy(f):
        at = pl.ds(pl.multiple_of(f * f_col, f_col), f_col)
        return pltpu.make_async_copy(w_in_hbm.at[:, at], w_in.at[:, at], win_sem.at[f])

    def w_out_copy(q):
        at = pl.ds(q * col, col)
        return pltpu.make_async_copy(w_out_hbm.at[:, at], w_out.at[:, at], wout_sem.at[q])

    tok_copy = pltpu.make_async_copy(tok_hbm, tok, tok_sem)
    tok_copy.start()
    for f in range(f_parts):
        w_in_copy(f).start()
    for q in range(parts):
        w_out_copy(q).start()

    barrier = pltpu.get_barrier_semaphore()
    for k in range(1, n_clu):
        pl.semaphore_signal(barrier, inc=1, device_id=(peer(k), grp), device_id_type=MESH)
    pl.semaphore_signal(barrier, inc=1, device_id=(clu, sib), device_id_type=MESH)
    for t in range(1, n_y):
        pl.semaphore_signal(barrier, inc=1, device_id=(clu, y_peer(t)), device_id_type=MESH)

    member[...] = (
        seg_ref[...] == lax.broadcasted_iota(jnp.int32, (docs, rows_n), 0)
    ).astype(F32).astype(BF16)
    sub = sub_ref[...]
    ones_at = lax.broadcasted_iota(jnp.int32, (docs, docs), 0) == lax.broadcasted_iota(
        jnp.int32, (docs, docs), 1
    )
    owner = jnp.sum(jnp.where(ones_at, owner_ref[...], 0), axis=0, keepdims=True)
    sub_col = jnp.sum(jnp.where(ones_at, sub, 0), axis=1, keepdims=True)
    hits = (lax.broadcasted_iota(jnp.int32, (n_clu, docs), 0) == owner).astype(F32)
    earlier = (
        lax.broadcasted_iota(jnp.int32, (docs, docs), 0)
        < lax.broadcasted_iota(jnp.int32, (docs, docs), 1)
    ).astype(F32).astype(BF16)
    before = jnp.dot(hits.astype(BF16), earlier, preferred_element_type=F32)
    slot = jnp.sum(before * hits, axis=0, keepdims=True).astype(jnp.int32)
    place[...] = (
        lax.broadcasted_iota(jnp.int32, (slots, docs), 0) == owner * cap + slot
    ).astype(F32).astype(BF16)
    lane = lax.broadcasted_iota(jnp.int32, (docs, META), 1)
    code = ((lane == sub_col // LO) | (lane == HI + lax.rem(sub_col, LO))).astype(F32)

    tok_copy.wait()
    blocks = 4
    block = rows_n // blocks

    @pl.loop(0, f_parts)
    def _(f):
        w_in_copy(f).wait()
        at = pl.ds(pl.multiple_of(f * f_col, f_col), f_col)
        bias = b_in_ref[:, at]

        def pre(r):
            return jnp.dot(
                tok[r * block:(r + 1) * block, :], w_in[:, at], preferred_element_type=F32
            )

        now = pre(0)
        for r in range(blocks):
            after = pre(r + 1) if r + 1 < blocks else None
            act[r * block:(r + 1) * block, at] = gelu(now + bias).astype(BF16)
            now = after

    def view(ref, part, g, at):
        return gath_meta.at[g, at] if part == parts else ref.at[g, part, at]

    def a_copy(part, k):
        source = send_meta if part == parts else send.at[part]
        return pltpu.make_async_remote_copy(
            src_ref=source.at[pl.ds(pl.multiple_of(peer(k) * cap, cap), cap)],
            dst_ref=view(gath, part, grp, pl.ds(pl.multiple_of(clu * cap, cap), cap)),
            send_sem=a_send.at[part, k], recv_sem=a_recv.at[part, k],
            device_id=(peer(k), grp), device_id_type=MESH,
        )

    every = pl.ds(0, slots)

    def f_copy(part, which, t):
        if which == "sib":
            g, to, s = grp, sib, 0
        elif which == "y":
            g, to, s = grp, y_peer(t), t
        else:
            g, to, s = y_source(t), sib, n_y - 1 + t
        return pltpu.make_async_remote_copy(
            src_ref=view(gath, part, g, every), dst_ref=view(gath, part, g, every),
            send_sem=f_send.at[part, s], recv_sem=f_recv.at[part, s],
            device_id=(clu, to), device_id_type=MESH,
        )

    def start_a(part, packed):
        source = send_meta if part == parts else send.at[part]
        source[...] = packed.astype(BF16)
        own = pl.ds(pl.multiple_of(clu * cap, cap), cap)
        mine = source[own, :]
        if part == parts:
            gath_meta[grp, own, :] = mine
        else:
            gath[grp, part, own, :] = mine
        for k in range(1, n_clu):
            a_copy(part, k).start()

    def turn(part):
        for k in range(1, n_clu):
            a_copy(part, k).wait_recv()
        for t in range(1, n_y):
            f_copy(part, "y", t).start()
        f_copy(part, "sib", 0).start()

    def pass_on(part):
        for t in range(1, n_y):
            f_copy(part, "y", t).wait_recv()
            f_copy(part, "on", t).start()

    counts = jnp.sum(member[...].astype(F32), axis=1, keepdims=True)
    squares = jnp.zeros((docs, 1), F32)
    for q in range(parts):
        w_out_copy(q).wait()
        at = slice(q * col, (q + 1) * col)
        totals = jnp.zeros((docs, col), F32)
        for r in range(blocks):
            rs = slice(r * block, (r + 1) * block)
            out = jnp.dot(act[rs, :], w_out[:, at], preferred_element_type=F32)
            out = (tok[rs, at].astype(F32) + out + b_out_ref[:, at]).astype(BF16)
            totals += jnp.dot(member[:, rs], out, preferred_element_type=F32)
        mean = totals / counts
        squares += jnp.sum(mean * mean, axis=1, keepdims=True)
        mean16 = mean.astype(BF16)
        pooled_ref[:, at] = mean16
        packed = jnp.dot(place[...], mean16, preferred_element_type=F32)
        if q == 0:
            pl.semaphore_wait(barrier, n_clu - 1 + n_y)
        start_a(q, packed)
        if q >= 2:
            turn(q - 2)
    inv = lax.rsqrt(squares + 1e-06)
    high = inv.astype(BF16).astype(F32)
    middle = (inv - high).astype(BF16).astype(F32)
    low = inv - high - middle
    norm_at = HI + LO
    meta = jnp.where(lane == norm_at, high, code)
    meta = jnp.where(lane == norm_at + 1, middle, meta)
    meta = jnp.where(lane == norm_at + 2, low, meta).astype(BF16)
    start_a(parts, jnp.dot(place[...], meta, preferred_element_type=F32))
    for part in range(max(0, parts - 2), parts + 1):
        turn(part)
    for part in range(parts + 1):
        pass_on(part)

    own_meta = gath_meta[grp]
    meta_lane = lax.broadcasted_iota(jnp.int32, (slots, META), 1)
    is_norm = (meta_lane >= norm_at) & (meta_lane < norm_at + 3)
    own_code = jnp.where(is_norm, 0.0, own_meta.astype(F32)).astype(BF16)
    pick_lane = lax.broadcasted_iota(jnp.int32, (8, META), 1)
    pick = ((pick_lane >= norm_at) & (pick_lane < norm_at + 3)).astype(F32).astype(BF16)
    own_inv = dot_nt(pick, own_meta)

    def best_of(g, itself):
        similar = jnp.zeros((slots, slots), F32)
        for q in range(parts):
            similar += dot_nt(gath[g, q], gath[grp, q])
        g_meta = gath_meta[g]
        inv_g = jnp.sum(jnp.where(is_norm, g_meta.astype(F32), 0.0), axis=1, keepdims=True)
        matched = dot_nt(g_meta, own_code) > 1.5
        if itself:
            matched = matched & (
                lax.broadcasted_iota(jnp.int32, (slots, slots), 0)
                != lax.broadcasted_iota(jnp.int32, (slots, slots), 1)
            )
        values = jnp.where(matched, similar * inv_g * own_inv[0:1, :], -1.0)
        return jnp.max(values, axis=0, keepdims=True)

    best = jnp.maximum(best_of(grp, True), -1.0)
    for part in range(parts + 1):
        f_copy(part, "sib", 0).wait_recv()
    best = jnp.maximum(best, best_of(sib, False))
    for t in range(1, n_y):
        best = jnp.maximum(best, best_of(y_source(t), False))
    for t in range(1, n_y):
        for part in range(parts + 1):
            f_copy(part, "on", t).wait_recv()
        best = jnp.maximum(best, best_of(y_source_sib(t), False))

    ret_out[...] = jnp.broadcast_to(best, (8, slots))
    ret_in[clu] = jnp.broadcast_to(best, (8, slots))

    def r_copy(k):
        return pltpu.make_async_remote_copy(
            src_ref=ret_out, dst_ref=ret_in.at[clu],
            send_sem=r_send.at[k], recv_sem=r_recv.at[k],
            device_id=(peer(k), grp), device_id_type=MESH,
        )

    for k in range(1, n_clu):
        r_copy(k).start()
    for part in range(parts + 1):
        for k in range(1, n_clu):
            a_copy(part, k).wait_send()
        f_copy(part, "sib", 0).wait_send()
        for t in range(1, n_y):
            f_copy(part, "y", t).wait_send()
            f_copy(part, "on", t).wait_send()
    for k in range(1, n_clu):
        r_copy(k).wait_recv()
    took = (
        lax.broadcasted_iota(jnp.int32, (slots, docs), 0) == clu * cap + slot
    ).astype(F32)
    got = jnp.concatenate([ret_in[c, 0:1, :] for c in range(n_clu)], axis=0)
    spread = jnp.dot(got, took, preferred_element_type=F32, precision=lax.Precision.HIGHEST)
    near_ref[...] = jnp.sum(spread * hits, axis=0, keepdims=True)
    for k in range(1, n_clu):
        r_copy(k).wait_send()


def per_device(tokens, segment_ids, w_in, b_in, w_out, b_out, owner_ids, sub_ids):
    n_clu = lax.axis_size("clu")
    n_grp = lax.axis_size("grp")
    docs = owner_ids.shape[0]
    rows_n, width = tokens.shape
    ff = w_in.shape[1]
    cap = max(16, 2 * docs // n_clu)
    slots = n_clu * cap
    parts = 4
    f_parts = 4
    n_y = n_grp // 2
    vmem = pl.BlockSpec(memory_space=pltpu.VMEM)
    hbm = pl.BlockSpec(memory_space=pl.ANY)
    dma = pltpu.SemaphoreType.DMA
    pooled, near = pl.pallas_call(
        functools.partial(kernel, n_clu, n_grp, cap, parts),
        out_shape=(
            jax.ShapeDtypeStruct((docs, width), BF16),
            jax.ShapeDtypeStruct((1, docs), F32),
        ),
        in_specs=[hbm, vmem, hbm, vmem, hbm, vmem, vmem, vmem],
        out_specs=(vmem, vmem),
        scratch_shapes=[
            pltpu.VMEM((rows_n, width), BF16),
            pltpu.VMEM((width, ff), BF16),
            pltpu.VMEM((ff, width), BF16),
            pltpu.VMEM((rows_n, ff), BF16),
            pltpu.VMEM((docs, rows_n), BF16),
            pltpu.VMEM((slots, docs), BF16),
            pltpu.VMEM((parts, slots, width // parts), BF16),
            pltpu.VMEM((slots, META), BF16),
            pltpu.VMEM((n_grp, parts, slots, width // parts), BF16),
            pltpu.VMEM((n_grp, slots, META), BF16),
            pltpu.VMEM((8, slots), F32),
            pltpu.VMEM((n_clu, 8, slots), F32),
            dma(()),
            dma((f_parts,)),
            dma((parts,)),
            dma((parts + 1, n_clu)),
            dma((parts + 1, n_clu)),
            dma((parts + 1, 2 * n_y)),
            dma((parts + 1, 2 * n_y)),
            dma((n_clu,)),
            dma((n_clu,)),
        ],
        compiler_params=pltpu.CompilerParams(
            collective_id=0, has_side_effects=True, vmem_limit_bytes=56 * 1024 * 1024
        ),
    )(
        tokens, segment_ids, w_in, b_in.reshape(1, ff), w_out, b_out.reshape(1, width),
        owner_ids, sub_ids.reshape(1, docs),
    )
    return (pooled, near.reshape(docs))


def solution(mesh):
    in_specs = (
        P(("clu", "grp"), None),
        P(("clu", "grp"), None),
        P(),
        P(),
        P(),
        P(),
        P(("clu", "grp"), None),
        P(("clu", "grp")),
    )
    out_specs = (P(("clu", "grp"), None), P(("clu", "grp")))
    return jax.shard_map(
        per_device, mesh=mesh, in_specs=in_specs, out_specs=out_specs, check_vma=False
    )
```

time: 143 us -> 49.9 us (0.35)
  waiting for transfers between devices: 58.5 us -> 0 us
  Pallas kernels: 0 us -> 44.8 us
  matrix products: 34.1 us -> 0 us
  starting transfers between devices: 15.5 us -> 0 us
  between operations: 14.2 us -> 0.64 us
  blocking collectives: 6.36 us -> 0 us
  local copies, waits for them, and re-layouts: 10.4 us -> 4.19 us
  other arithmetic: 3.35 us -> 0 us
    all_to_all x3 -> x0, waiting for transfers between devices: 54.8 us -> none  [the longest x1 48.4 us: per_device(): lax.all_to_all(send_units.reshape(n_clu, n_grp * capacity, model_width),...]
    pallas_call x0 -> x1, Pallas kernels: none -> 44.8 us  [per_device(): pl.pallas_call(functools.partial(kernel, n_clu, n_grp, cap, parts), out_s...]
    dot_general x3 -> x0, matrix products: 34.1 us -> none  [the longest x1 30.1 us: encode(): jnp.dot(activated, w_out, preferred_element_type=jnp.float32)]
    all_to_all x3 -> x0, starting transfers between devices: 15.4 us -> none  [the longest x1 6.26 us: per_device(): lax.all_to_all(send_meta.reshape(n_clu, n_grp * capacity, 2), 'clu', spli...]
    scatter x2 -> x0, local copies, waits for them, and re-layouts: 6.66 us -> none  [the longest x1 4.82 us: per_device(): send_units = jnp.zeros((n_clu * n_grp * capacity, model_width), jnp.bfloa...]
    all_gather x1 -> x0, blocking collectives: 6.36 us -> none  [per_device(): lax.all_gather(doc_info, 'grp', axis=0, tiled=True)]
    unnamed x10 -> x3, local copies, waits for them, and re-layouts: 0.03 us -> 4.19 us
    all_gather x1 -> x0, waiting for transfers between devices: 3.62 us -> none  [per_device(): lax.all_gather(unit_rows, 'grp', axis=0, tiled=True)]
  transfers between devices with their start and end apart: 4 -> 0, of which waited for: 3 -> 0; matrix products, arithmetic and copies ran while one was open for 6% -> 0% of each run, Pallas kernels for 0% -> 0%
where the time goes in v1:
time: 49.9 us; the launch traced here: 49.7 us
  Pallas kernels  44.8 us (90%)
  local copies, waits for them, and re-layouts  4.19 us (8%)
  between operations  0.64 us (1%)
    pallas_call x1, Pallas kernels, per_device(): pl.pallas_call(functools.partial(kernel, n_clu, n_grp, cap, parts), out_s...  44.8 us
    unnamed x3, local copies, waits for them, and re-layouts  4.19 us

profile of v1, /device:TPU:0, one launch (start us, length us, event | category | flops | bytes accessed | tf_op | source)
XLA Modules:
  0.0 49.7 jit_solution(12234778689329346877)
XLA Ops:
  0.6 1.4 %copy.10.owner_ref = s32[128,1]{1,0:T(8,128)} copy(s32[128,1]{0,1:T(1,128)} %param.14) | data formatting | bytes 1024 | tf_op args[6]
  2.0 44.8 %shard_map.95 = (bf16[128,1024]{1,0:T(8,128)(2,1)}, f32[1,128]{1,0:T(1,128)}) custom-call(bf16[1024,1024]{1,0:T(8,128)(2,1)} %tok_hbm.1, s32[1,1024]{1,0:T(1,128)} %seg_ref.1, bf16[1024,2048]{1,0:T(8,128)(2,1)} %w_in_hbm.1, f32[1,2048]{1,0:T(1,128)} %bitcast.4, bf16[2048,1024]{1,0:T(8,128)(2,1)} %w_out_hbm.1, f32[1,1024]{1,0:T(1,128)} %bitcast.5, ...), custom_call_target="tpu_custom_call" | custom-call | tf_op jit(solution)/shard_map/pallas_call | solution.py:288
  46.9 1.7 %copy.13 = bf16[128,1024]{1,0:T(8,128)(2,1)} copy(bf16[128,1024]{1,0:T(8,128)(2,1)} %get-tuple-element.8) | data formatting | bytes 524288
  48.5 1.1 %copy.14 = f32[128]{0:T(128)} copy(f32[128]{0:T(128)} %bitcast.7) | data formatting | bytes 1024

commit v2 on v1

--- a/solution.py
+++ b/solution.py
@@ -15,7 +15,13 @@
 
 
 def gelu(x):
-    return 0.5 * x * (1.0 + lax.erf(x * 0.7071067811865476))
+    size = jnp.abs(x)
+    t = 1.0 / (1.0 + 0.23164190091 * size)
+    tail = 0.5307027145
+    for term in (-0.7265760135, 0.7107068705, -0.142248368, 0.127414796):
+        tail = tail * t + term
+    tail = tail * t * size * jnp.exp2(x * x * -0.72134752044448)
+    return jnp.maximum(x, 0.0) - tail
 
 
 def dot_nt(a, b):
@@ -84,7 +90,7 @@
     ones_at = lax.broadcasted_iota(jnp.int32, (docs, docs), 0) == lax.broadcasted_iota(
         jnp.int32, (docs, docs), 1
     )
-    owner = jnp.sum(jnp.where(ones_at, owner_ref[...], 0), axis=0, keepdims=True)
+    owner = owner_ref[...]
     sub_col = jnp.sum(jnp.where(ones_at, sub, 0), axis=1, keepdims=True)
     hits = (lax.broadcasted_iota(jnp.int32, (n_clu, docs), 0) == owner).astype(F32)
     earlier = (
@@ -97,28 +103,7 @@
         lax.broadcasted_iota(jnp.int32, (slots, docs), 0) == owner * cap + slot
     ).astype(F32).astype(BF16)
     lane = lax.broadcasted_iota(jnp.int32, (docs, META), 1)
-    code = ((lane == sub_col // LO) | (lane == HI + lax.rem(sub_col, LO))).astype(F32)
-
-    tok_copy.wait()
-    blocks = 4
-    block = rows_n // blocks
-
-    @pl.loop(0, f_parts)
-    def _(f):
-        w_in_copy(f).wait()
-        at = pl.ds(pl.multiple_of(f * f_col, f_col), f_col)
-        bias = b_in_ref[:, at]
-
-        def pre(r):
-            return jnp.dot(
-                tok[r * block:(r + 1) * block, :], w_in[:, at], preferred_element_type=F32
-            )
-
-        now = pre(0)
-        for r in range(blocks):
-            after = pre(r + 1) if r + 1 < blocks else None
-            act[r * block:(r + 1) * block, at] = gelu(now + bias).astype(BF16)
-            now = after
+    code = ((lane == sub_col // LO) | (lane == HI + lax.rem(sub_col, LO))).astype(F32).astype(BF16)
 
     def view(ref, part, g, at):
         return gath_meta.at[g, at] if part == parts else ref.at[g, part, at]
@@ -170,9 +155,32 @@
         for t in range(1, n_y):
             f_copy(part, "y", t).wait_recv()
             f_copy(part, "on", t).start()
-
+    pl.semaphore_wait(barrier, n_clu - 1 + n_y)
+    start_a(parts, jnp.dot(place[...], code, preferred_element_type=F32))
+
+    tok_copy.wait()
+    blocks = 4
+    block = rows_n // blocks
+
+    @pl.loop(0, f_parts)
+    def _(f):
+        w_in_copy(f).wait()
+        at = pl.ds(pl.multiple_of(f * f_col, f_col), f_col)
+        bias = b_in_ref[:, at]
+
+        def pre(r):
+            return jnp.dot(
+                tok[r * block:(r + 1) * block, :], w_in[:, at], preferred_element_type=F32
+            )
+
+        now = pre(0)
+        for r in range(blocks):
+            after = pre(r + 1) if r + 1 < blocks else None
+            act[r * block:(r + 1) * block, at] = gelu(now + bias).astype(BF16)
+            now = after
+
+    turn(parts)
     counts = jnp.sum(member[...].astype(F32), axis=1, keepdims=True)
-    squares = jnp.zeros((docs, 1), F32)
     for q in range(parts):
         w_out_copy(q).wait()
         at = slice(q * col, (q + 1) * col)
@@ -183,62 +191,61 @@
             out = (tok[rs, at].astype(F32) + out + b_out_ref[:, at]).astype(BF16)
             totals += jnp.dot(member[:, rs], out, preferred_element_type=F32)
         mean = totals / counts
-        squares += jnp.sum(mean * mean, axis=1, keepdims=True)
         mean16 = mean.astype(BF16)
         pooled_ref[:, at] = mean16
         packed = jnp.dot(place[...], mean16, preferred_element_type=F32)
+        start_a(q, packed)
         if q == 0:
-            pl.semaphore_wait(barrier, n_clu - 1 + n_y)
-        start_a(q, packed)
+            pass_on(parts)
         if q >= 2:
             turn(q - 2)
-    inv = lax.rsqrt(squares + 1e-06)
-    high = inv.astype(BF16).astype(F32)
-    middle = (inv - high).astype(BF16).astype(F32)
-    low = inv - high - middle
-    norm_at = HI + LO
-    meta = jnp.where(lane == norm_at, high, code)
-    meta = jnp.where(lane == norm_at + 1, middle, meta)
-    meta = jnp.where(lane == norm_at + 2, low, meta).astype(BF16)
-    start_a(parts, jnp.dot(place[...], meta, preferred_element_type=F32))
-    for part in range(max(0, parts - 2), parts + 1):
+    for part in range(max(0, parts - 2), parts):
         turn(part)
-    for part in range(parts + 1):
+    for part in range(parts - 1):
         pass_on(part)
 
-    own_meta = gath_meta[grp]
-    meta_lane = lax.broadcasted_iota(jnp.int32, (slots, META), 1)
-    is_norm = (meta_lane >= norm_at) & (meta_lane < norm_at + 3)
-    own_code = jnp.where(is_norm, 0.0, own_meta.astype(F32)).astype(BF16)
-    pick_lane = lax.broadcasted_iota(jnp.int32, (8, META), 1)
-    pick = ((pick_lane >= norm_at) & (pick_lane < norm_at + 3)).astype(F32).astype(BF16)
-    own_inv = dot_nt(pick, own_meta)
-
-    def best_of(g, itself):
+    own_code = gath_meta[grp]
+    diagonal = lax.broadcasted_iota(jnp.int32, (slots, slots), 0) == lax.broadcasted_iota(
+        jnp.int32, (slots, slots), 1
+    )
+
+    def products(g):
         similar = jnp.zeros((slots, slots), F32)
         for q in range(parts):
             similar += dot_nt(gath[g, q], gath[grp, q])
-        g_meta = gath_meta[g]
-        inv_g = jnp.sum(jnp.where(is_norm, g_meta.astype(F32), 0.0), axis=1, keepdims=True)
-        matched = dot_nt(g_meta, own_code) > 1.5
-        if itself:
-            matched = matched & (
-                lax.broadcasted_iota(jnp.int32, (slots, slots), 0)
-                != lax.broadcasted_iota(jnp.int32, (slots, slots), 1)
-            )
-        values = jnp.where(matched, similar * inv_g * own_inv[0:1, :], -1.0)
+        return similar
+
+    def inverse(squares):
+        return lax.rsqrt(squares + 1e-06)
+
+    def matches(g):
+        return dot_nt(gath_meta[g], own_code) > 1.5
+
+    similar = products(grp)
+    own_squares = jnp.where(diagonal, similar, 0.0)
+    across = inverse(jnp.sum(own_squares, axis=0, keepdims=True))
+    down = inverse(jnp.sum(own_squares, axis=1, keepdims=True))
+    values = jnp.where(matches(grp) & ~diagonal, similar * down * across, -1.0)
+    best = jnp.maximum(jnp.max(values, axis=0, keepdims=True), -1.0)
+
+    def best_of(g):
+        squares = jnp.zeros((slots, 1), F32)
+        for q in range(parts):
+            rows = gath[g, q].astype(F32)
+            squares += jnp.sum(rows * rows, axis=1, keepdims=True)
+        values = jnp.where(matches(g), products(g) * inverse(squares) * across, -1.0)
         return jnp.max(values, axis=0, keepdims=True)
 
-    best = jnp.maximum(best_of(grp, True), -1.0)
     for part in range(parts + 1):
         f_copy(part, "sib", 0).wait_recv()
-    best = jnp.maximum(best, best_of(sib, False))
+    best = jnp.maximum(best, best_of(sib))
+    pass_on(parts - 1)
     for t in range(1, n_y):
-        best = jnp.maximum(best, best_of(y_source(t), False))
+        best = jnp.maximum(best, best_of(y_source(t)))
     for t in range(1, n_y):
         for part in range(parts + 1):
             f_copy(part, "on", t).wait_recv()
-        best = jnp.maximum(best, best_of(y_source_sib(t), False))
+        best = jnp.maximum(best, best_of(y_source_sib(t)))
 
     ret_out[...] = jnp.broadcast_to(best, (8, slots))
     ret_in[clu] = jnp.broadcast_to(best, (8, slots))
@@ -321,7 +328,7 @@
         ),
     )(
         tokens, segment_ids, w_in, b_in.reshape(1, ff), w_out, b_out.reshape(1, width),
-        owner_ids, sub_ids.reshape(1, docs),
+        owner_ids.reshape(1, docs), sub_ids.reshape(1, docs),
     )
     return (pooled, near.reshape(docs))
 

time: 49.9 us -> 50.1 us (level)
  Pallas kernels: 44.8 us -> 46.5 us
  local copies, waits for them, and re-layouts: 4.19 us -> 2.8 us
    pallas_call x1, Pallas kernels: 44.8 us -> 46.5 us  [per_device(): pl.pallas_call(functools.partial(kernel, n_clu, n_grp, cap, parts), out_s...]
    unnamed x3 -> x2, local copies, waits for them, and re-layouts: 4.19 us -> 2.8 us
where the time goes in v2:
time: 50.1 us; the launch traced here: 49.9 us
  Pallas kernels  46.5 us (93%)
  local copies, waits for them, and re-layouts  2.8 us (6%)
  between operations  0.64 us (1%)
    pallas_call x1, Pallas kernels, per_device(): pl.pallas_call(functools.partial(kernel, n_clu, n_grp, cap, parts), out_s...  46.5 us
    unnamed x2, local copies, waits for them, and re-layouts  2.8 us

profile of v2, /device:TPU:0, one launch (start us, length us, event | category | flops | bytes accessed | tf_op | source)
XLA Modules:
  0.0 49.9 jit_solution(316418925432564814)
XLA Ops:
  0.6 46.5 %shard_map.95 = (bf16[128,1024]{1,0:T(8,128)(2,1)}, f32[1,128]{1,0:T(1,128)}) custom-call(bf16[1024,1024]{1,0:T(8,128)(2,1)} %tok_hbm.1, s32[1,1024]{1,0:T(1,128)} %seg_ref.1, bf16[1024,2048]{1,0:T(8,128)(2,1)} %w_in_hbm.1, f32[1,2048]{1,0:T(1,128)} %bitcast.5, bf16[2048,1024]{1,0:T(8,128)(2,1)} %w_out_hbm.1, f32[1,1024]{1,0:T(1,128)} %bitcast.6, ...), custom_call_target="tpu_custom_call" | custom-call | tf_op jit(solution)/shard_map/pallas_call | solution.py:295
  47.1 1.7 %copy.12 = bf16[128,1024]{1,0:T(8,128)(2,1)} copy(bf16[128,1024]{1,0:T(8,128)(2,1)} %get-tuple-element.8) | data formatting | bytes 524288
  48.8 1.1 %copy.13 = f32[128]{0:T(128)} copy(f32[128]{0:T(128)} %bitcast.9) | data formatting | bytes 1024

commit v3 on v1

--- a/solution.py
+++ b/solution.py
@@ -84,7 +84,7 @@
     ones_at = lax.broadcasted_iota(jnp.int32, (docs, docs), 0) == lax.broadcasted_iota(
         jnp.int32, (docs, docs), 1
     )
-    owner = jnp.sum(jnp.where(ones_at, owner_ref[...], 0), axis=0, keepdims=True)
+    owner = owner_ref[...]
     sub_col = jnp.sum(jnp.where(ones_at, sub, 0), axis=1, keepdims=True)
     hits = (lax.broadcasted_iota(jnp.int32, (n_clu, docs), 0) == owner).astype(F32)
     earlier = (
@@ -203,7 +203,7 @@
     start_a(parts, jnp.dot(place[...], meta, preferred_element_type=F32))
     for part in range(max(0, parts - 2), parts + 1):
         turn(part)
-    for part in range(parts + 1):
+    for part in range(parts - 1):
         pass_on(part)
 
     own_meta = gath_meta[grp]
@@ -233,6 +233,8 @@
     for part in range(parts + 1):
         f_copy(part, "sib", 0).wait_recv()
     best = jnp.maximum(best, best_of(sib, False))
+    for part in range(parts - 1, parts + 1):
+        pass_on(part)
     for t in range(1, n_y):
         best = jnp.maximum(best, best_of(y_source(t), False))
     for t in range(1, n_y):
@@ -321,7 +323,7 @@
         ),
     )(
         tokens, segment_ids, w_in, b_in.reshape(1, ff), w_out, b_out.reshape(1, width),
-        owner_ids, sub_ids.reshape(1, docs),
+        owner_ids.reshape(1, docs), sub_ids.reshape(1, docs),
     )
     return (pooled, near.reshape(docs))
 

time: 49.9 us -> 47.7 us (0.956)
  local copies, waits for them, and re-layouts: 4.19 us -> 2.8 us
  Pallas kernels: 44.8 us -> 44 us
    unnamed x3 -> x2, local copies, waits for them, and re-layouts: 4.19 us -> 2.8 us
    pallas_call x1, Pallas kernels: 44.8 us -> 44 us  [per_device(): pl.pallas_call(functools.partial(kernel, n_clu, n_grp, cap, parts), out_s...]
where the time goes in v3:
time: 47.7 us; the launch traced here: 47.5 us
  Pallas kernels  44 us (92%)
  local copies, waits for them, and re-layouts  2.8 us (6%)
  between operations  0.64 us (1%)
    pallas_call x1, Pallas kernels, per_device(): pl.pallas_call(functools.partial(kernel, n_clu, n_grp, cap, parts), out_s...  44 us
    unnamed x2, local copies, waits for them, and re-layouts  2.8 us

profile of v3, /device:TPU:0, one launch (start us, length us, event | category | flops | bytes accessed | tf_op | source)
XLA Modules:
  0.0 47.5 jit_solution(7538514125054008542)
XLA Ops:
  0.6 44.0 %shard_map.95 = (bf16[128,1024]{1,0:T(8,128)(2,1)}, f32[1,128]{1,0:T(1,128)}) custom-call(bf16[1024,1024]{1,0:T(8,128)(2,1)} %tok_hbm.1, s32[1,1024]{1,0:T(1,128)} %seg_ref.1, bf16[1024,2048]{1,0:T(8,128)(2,1)} %w_in_hbm.1, f32[1,2048]{1,0:T(1,128)} %bitcast.5, bf16[2048,1024]{1,0:T(8,128)(2,1)} %w_out_hbm.1, f32[1,1024]{1,0:T(1,128)} %bitcast.6, ...), custom_call_target="tpu_custom_call" | custom-call | tf_op jit(solution)/shard_map/pallas_call | solution.py:290
  44.7 1.7 %copy.12 = bf16[128,1024]{1,0:T(8,128)(2,1)} copy(bf16[128,1024]{1,0:T(8,128)(2,1)} %get-tuple-element.8) | data formatting | bytes 524288
  46.3 1.1 %copy.13 = f32[128]{0:T(128)} copy(f32[128]{0:T(128)} %bitcast.9) | data formatting | bytes 1024

commit v4 on v3

--- a/solution.py
+++ b/solution.py
@@ -15,7 +15,15 @@
 
 
 def gelu(x):
-    return 0.5 * x * (1.0 + lax.erf(x * 0.7071067811865476))
+    size = jnp.abs(x)
+    below = 1.0 + 0.23164190091 * size
+    t = pl.reciprocal(below, approx=True)
+    t = t * (2.0 - below * t)
+    tail = 0.5307027145
+    for term in (-0.7265760135, 0.7107068705, -0.142248368, 0.127414796):
+        tail = tail * t + term
+    tail = tail * t * size * jnp.exp2(x * x * -0.72134752044448)
+    return jnp.maximum(x, 0.0) - tail
 
 
 def dot_nt(a, b):

time: 47.7 us -> 52.9 us (1.11)
  Pallas kernels: 44 us -> 49.2 us
    pallas_call x1, Pallas kernels: 44 us -> 49.2 us  [per_device(): pl.pallas_call(functools.partial(kernel, n_clu, n_grp, cap, parts), out_s...]
where the time goes in v4:
time: 52.9 us; the launch traced here: 52.7 us
  Pallas kernels  49.2 us (93%)
  local copies, waits for them, and re-layouts  2.8 us (5%)
  between operations  0.64 us (1%)
    pallas_call x1, Pallas kernels, per_device(): pl.pallas_call(functools.partial(kernel, n_clu, n_grp, cap, parts), out_s...  49.2 us
    unnamed x2, local copies, waits for them, and re-layouts  2.8 us

profile of v4, /device:TPU:0, one launch (start us, length us, event | category | flops | bytes accessed | tf_op | source)
XLA Modules:
  0.0 52.7 jit_solution(1652460776341215043)
XLA Ops:
  0.6 49.2 %shard_map.95 = (bf16[128,1024]{1,0:T(8,128)(2,1)}, f32[1,128]{1,0:T(1,128)}) custom-call(bf16[1024,1024]{1,0:T(8,128)(2,1)} %tok_hbm.1, s32[1,1024]{1,0:T(1,128)} %seg_ref.1, bf16[1024,2048]{1,0:T(8,128)(2,1)} %w_in_hbm.1, f32[1,2048]{1,0:T(1,128)} %bitcast.5, bf16[2048,1024]{1,0:T(8,128)(2,1)} %w_out_hbm.1, f32[1,1024]{1,0:T(1,128)} %bitcast.6, ...), custom_call_target="tpu_custom_call" | custom-call | tf_op jit(solution)/shard_map/pallas_call | solution.py:298
  49.9 1.7 %copy.12 = bf16[128,1024]{1,0:T(8,128)(2,1)} copy(bf16[128,1024]{1,0:T(8,128)(2,1)} %get-tuple-element.8) | data formatting | bytes 524288
  51.5 1.1 %copy.13 = f32[128]{0:T(128)} copy(f32[128]{0:T(128)} %bitcast.9) | data formatting | bytes 1024
